TPU v7x, 32 devices: a whole 2x2x4 slice. The times are simulated.
32 devices in a mesh: ctx: 16 (over z, x, core), head: 2 (over y).
Axes of the slice: x: 2, y: 2, z: 4, core: 2. Of those that a mesh axis runs over, the one named last changes fastest.
Arguments:
- q_latent: bfloat16 [2048, 64, 512], P('ctx', 'head'), may hold values from -1.25 to 1.25
- q_rope: bfloat16 [2048, 4096], P('ctx', 'head'), may hold values from -1.25 to 1.25
- attn_out: bfloat16 [2048, 64, 512], P('ctx', 'head'), may hold values from -4 to 4
- grad_out: bfloat16 [2048, 64, 512], P('ctx', 'head'), may hold values from -1 to 1
- log_total: float32 [2048, 64], P('ctx', 'head'), may hold values from 4 to 6
- latent: bfloat16 [2048, 512], P('ctx'), may hold values from -2.5 to 2.5
- key_rope: bfloat16 [2048, 64], P('ctx'), may hold values from -2.5 to 2.5
- doc_start: int32 [2048], P('ctx'), may hold values from 0 to 2047, as said below
Outputs:
- grad_q_latent: bfloat16 [2048, 64, 512], P('ctx', 'head')
- grad_q_rope: bfloat16 [2048, 4096], P('ctx', 'head')
- grad_latent: bfloat16 [2048, 512], P(('ctx', 'head'))
- grad_key_rope: bfloat16 [2048, 64], P(('ctx', 'head'))
Inputs may be any that keep to these rules, and one draw needn't show every extreme that they name: doc_start[t] is the first token of the document that holds token t. Documents are runs of 1 to 897 tokens laid end to end from token 0; one document has exactly 897 tokens, and the last token of the sequence is a document of its own.
All inputs are finite; a program needn't handle non-finite values.
Results may differ from a plain program's by a relative error of at most 0.0056.
Values may be sent and summed in bfloat16 or wider, within the bound.
A program may use at most 128 MiB of HBM per device.

v0:
```python
import functools

import jax
import jax.numpy as jnp
from jax import lax
from jax.experimental import pallas as pl
from jax.experimental.pallas import tpu as pltpu
from jax.sharding import PartitionSpec as P

ROPE = 64
NOPE = 128
LEVELS = 3
SPAN = 2**LEVELS
SCALE = (NOPE + ROPE) ** (-0.5)
LOG2E = 1.4426950408889634
ORDER = (0, 3, 4, 5, 6, 7, 1, 2)
GROUP = 2
BLOCK = 512
HIDDEN = -1e30
MESH = pl.DeviceIdType.MESH


def dot_nt(a, b):
    return lax.dot_general(a, b, (((1,), (1,)), ((), ())), preferred_element_type=jnp.float32)


def dot_tn(a, b):
    return lax.dot_general(a, b, (((0,), (0,)), ((), ())), preferred_element_type=jnp.float32)


def dot_nn(a, b):
    return lax.dot_general(a, b, (((1,), (0,)), ((), ())), preferred_element_type=jnp.float32)


def kernel(
    n_ctx,
    n_head,
    tok,
    heads,
    lat,
    q_hbm,
    qr_hbm,
    ao_hbm,
    go_hbm,
    lt_hbm,
    kv_own,
    starts,
    gq_hbm,
    gqr_hbm,
    gkv_out,
    q,
    qr,
    go,
    ao,
    lt,
    delta,
    kv,
    bias,
    acc,
    gacc,
    part,
    recv,
    total,
    gq,
    gqr,
    in_sem,
    out_sem,
    kv_send,
    kv_recv,
    p_send,
    p_recv,
):
    me = lax.axis_index("ctx")
    my_head = lax.axis_index("head")
    rows = tok * heads
    block = min(BLOCK, rows)
    count = rows // block
    tok_blk = block // heads
    piece = tok // n_head
    width = GROUP * tok
    slot_of = {dist: place for place, dist in enumerate(ORDER)}

    barrier = pltpu.get_barrier_semaphore()
    for dist in range(-(SPAN - 1), SPAN):
        for turn in range(n_head):
            if dist == 0 and turn == 0:
                continue

            @pl.when((me + dist >= 0) & (me + dist < n_ctx))
            def _():
                pl.semaphore_signal(
                    barrier,
                    inc=1,
                    device_id=(me + dist, lax.rem(my_head + turn, n_head)),
                    device_id_type=MESH,
                )

    def load(b):
        rng = pl.ds(b * block, block)
        return [
            pltpu.make_async_copy(src.at[rng], dst.at[rng], in_sem.at[i, b])
            for i, (src, dst) in enumerate(
                ((go_hbm, go), (ao_hbm, ao), (q_hbm, q), (qr_hbm, qr), (lt_hbm, lt))
            )
        ]

    for b in range(count):
        for copy in load(b):
            copy.start()

    reach = jnp.minimum(me, SPAN - 1) + jnp.minimum(n_ctx - 1 - me, SPAN - 1) + 1
    pl.semaphore_wait(barrier, reach * n_head - 1)

    def kv_copy(dist):
        return pltpu.make_async_remote_copy(
            src_ref=kv_own,
            dst_ref=kv.at[pl.ds(slot_of[dist] * tok, tok)],
            send_sem=kv_send.at[dist],
            recv_sem=kv_recv.at[dist],
            device_id=(me + dist, my_head),
            device_id_type=MESH,
        )

    for dist in ORDER[1:]:

        @pl.when(me + dist < n_ctx)
        def _():
            kv_copy(dist).start()

    kv[pl.ds(0, tok)] = kv_own[...]
    for dist in ORDER[1:]:

        @pl.when(me < dist)
        def _():
            kv[pl.ds(slot_of[dist] * tok, tok)] = jnp.zeros((tok, kv.shape[1]), kv.dtype)

    query_pos = me * tok + lax.broadcasted_iota(jnp.int32, (tok, tok), 0)
    lane = lax.broadcasted_iota(jnp.int32, (tok, tok), 1)
    for place, dist in enumerate(ORDER):
        key_pos = (me - dist) * tok + lane
        seen = (key_pos >= starts[...]) & (key_pos <= query_pos)
        bias[place // GROUP, :, pl.ds((place % GROUP) * tok, tok)] = jnp.where(seen, 0.0, HIDDEN)

    def part_copy(dist, turn):
        target = lax.rem(my_head + turn, n_head)
        return pltpu.make_async_remote_copy(
            src_ref=part.at[pl.ds(pl.multiple_of(slot_of[dist] * tok + target * piece, piece), piece)],
            dst_ref=recv.at[dist * n_head + turn],
            send_sem=p_send.at[dist * n_head + turn],
            recv_sem=p_recv.at[dist * n_head + turn],
            device_id=(me - dist, target),
            device_id_type=MESH,
        )

    groups = SPAN // GROUP
    for g in range(groups):
        for dist in ORDER[g * GROUP : (g + 1) * GROUP]:
            if dist:

                @pl.when(me >= dist)
                def _():
                    kv_copy(dist).wait_recv()

        gacc[...] = jnp.zeros_like(gacc)

        def step(b, unused):
            start = pl.multiple_of(b * block, block)
            rng = pl.ds(start, block)
            if g == 0:
                for copy in load(b):
                    copy.wait()
                d = jnp.sum(
                    go[rng, :].astype(jnp.float32) * ao[rng, :].astype(jnp.float32),
                    axis=1,
                    keepdims=True,
                )
                delta[rng, :] = jnp.broadcast_to(d * SCALE, (block, 128))
            keys = kv[pl.ds(g * width, width), :]
            q_b, qr_b, go_b = q[rng, :], qr[rng, :], go[rng, :]
            scores = dot_nt(q_b, keys[:, :lat]) + dot_nt(qr_b, keys[:, lat:])
            grad_probs = dot_nt(go_b, keys[:, :lat])
            hide = bias[g, pl.ds(pl.multiple_of(b * tok_blk, tok_blk), tok_blk), :]
            hide = jnp.broadcast_to(hide[:, None, :], (tok_blk, heads, width)).reshape(block, width)
            times = width // 128
            lt_b = jnp.concatenate([lt[rng, :]] * times, axis=1)
            d_b = jnp.concatenate([delta[rng, :]] * times, axis=1)
            probs = jnp.exp2(scores * (SCALE * LOG2E) - lt_b + hide)
            grads = probs * (grad_probs * SCALE - d_b)
            probs_b = probs.astype(jnp.bfloat16)
            grad_b = grads.astype(jnp.bfloat16)
            gq_b = dot_nn(grad_b, keys)
            if g > 0:
                gq_b = acc[rng, :] + gq_b
            if g < groups - 1:
                acc[rng, :] = gq_b
            else:
                gq[rng, :] = gq_b[:, :lat].astype(jnp.bfloat16)
                gqr[rng, :] = gq_b[:, lat:].astype(jnp.bfloat16)
                pltpu.make_async_copy(gq.at[rng], gq_hbm.at[rng], out_sem.at[0, b]).start()
                pltpu.make_async_copy(gqr.at[rng], gqr_hbm.at[rng], out_sem.at[1, b]).start()
            gacc[:, :lat] += dot_tn(probs_b, go_b) + dot_tn(grad_b, q_b)
            gacc[:, lat:] += dot_tn(grad_b, qr_b)
            return unused

        lax.fori_loop(0, count, step, 0)
        part[pl.ds(g * width, width), :] = gacc[...].astype(jnp.bfloat16)
        for dist in ORDER[g * GROUP : (g + 1) * GROUP]:
            for turn in range(n_head):
                if dist == 0 and turn == 0:
                    continue

                @pl.when(me >= dist)
                def _():
                    part_copy(dist, turn).start()

    total[...] = part[pl.ds(pl.multiple_of(my_head * piece, piece), piece), :].astype(jnp.float32)
    for dist in ORDER:
        for turn in range(n_head):
            if dist == 0 and turn == 0:
                continue

            @pl.when(me + dist < n_ctx)
            def _():
                part_copy(dist, turn).wait_recv()
                total[...] += recv[dist * n_head + turn].astype(jnp.float32)

    gkv_out[...] = total[...].astype(jnp.bfloat16)
    for dist in ORDER:

        if dist:

            @pl.when(me + dist < n_ctx)
            def _():
                kv_copy(dist).wait_send()

        for turn in range(n_head):
            if dist == 0 and turn == 0:
                continue

            @pl.when(me >= dist)
            def _():
                part_copy(dist, turn).wait_send()

    for b in range(count):
        rng = pl.ds(b * block, block)
        pltpu.make_async_copy(gq.at[rng], gq_hbm.at[rng], out_sem.at[0, b]).wait()
        pltpu.make_async_copy(gqr.at[rng], gqr_hbm.at[rng], out_sem.at[1, b]).wait()


def local(q_latent, q_rope, attn_out, grad_out, log_total, latent, key_rope, doc_start):
    n_ctx, n_head = lax.axis_size("ctx"), lax.axis_size("head")
    tok, heads, lat = q_latent.shape
    rows = tok * heads
    rope = key_rope.shape[1]
    wide = lat + 128
    block = min(BLOCK, rows)
    count = rows // block
    piece = tok // n_head
    width = GROUP * tok
    qr = jnp.pad(q_rope.reshape(rows, rope), ((0, 0), (0, 128 - rope)))
    kv = jnp.concatenate([latent, jnp.pad(key_rope, ((0, 0), (0, 128 - rope)))], axis=1)
    lt = jnp.broadcast_to((log_total * LOG2E).reshape(rows, 1), (rows, 128))
    starts = jnp.broadcast_to(doc_start[:, None], (tok, tok))
    bf, f32 = jnp.bfloat16, jnp.float32
    hbm = pl.BlockSpec(memory_space=pl.ANY)
    vmem = pl.BlockSpec(memory_space=pltpu.VMEM)
    gq, gqr, gkv = pl.pallas_call(
        functools.partial(kernel, n_ctx, n_head, tok, heads, lat),
        out_shape=(
            jax.ShapeDtypeStruct((rows, lat), bf),
            jax.ShapeDtypeStruct((rows, 128), bf),
            jax.ShapeDtypeStruct((piece, wide), bf),
        ),
        in_specs=[hbm] * 5 + [vmem] * 2,
        out_specs=(hbm, hbm, vmem),
        scratch_shapes=[
            pltpu.VMEM((rows, lat), bf),
            pltpu.VMEM((rows, 128), bf),
            pltpu.VMEM((rows, lat), bf),
            pltpu.VMEM((rows, lat), bf),
            pltpu.VMEM((rows, 128), f32),
            pltpu.VMEM((rows, 128), f32),
            pltpu.VMEM((SPAN * tok, wide), bf),
            pltpu.VMEM((SPAN // GROUP, tok, width), f32),
            pltpu.VMEM((rows, wide), f32),
            pltpu.VMEM((width, wide), f32),
            pltpu.VMEM((SPAN * tok, wide), bf),
            pltpu.VMEM((SPAN * n_head, piece, wide), bf),
            pltpu.VMEM((piece, wide), f32),
            pltpu.VMEM((rows, lat), bf),
            pltpu.VMEM((rows, 128), bf),
            pltpu.SemaphoreType.DMA((5, count)),
            pltpu.SemaphoreType.DMA((2, count)),
            pltpu.SemaphoreType.DMA((SPAN,)),
            pltpu.SemaphoreType.DMA((SPAN,)),
            pltpu.SemaphoreType.DMA((SPAN * n_head,)),
            pltpu.SemaphoreType.DMA((SPAN * n_head,)),
        ],
        compiler_params=pltpu.CompilerParams(
            collective_id=0, has_side_effects=True, vmem_limit_bytes=56 * 2**20
        ),
    )(
        q_latent.reshape(rows, lat),
        qr,
        attn_out.reshape(rows, lat),
        grad_out.reshape(rows, lat),
        lt,
        kv,
        starts,
    )
    return (
        gq.reshape(tok, heads, lat),
        gqr[:, :rope].reshape(tok, heads * rope),
        gkv[:, :lat],
        gkv[:, lat : lat + rope],
    )


def solution(mesh):
    in_specs = (
        P("ctx", "head", None),
        P("ctx", "head"),
        P("ctx", "head", None),
        P("ctx", "head", None),
        P("ctx", "head"),
        P("ctx", None),
        P("ctx", None),
        P("ctx"),
    )
    out_specs = (
        P("ctx", "head", None),
        P("ctx", "head"),
        P(("ctx", "head"), None),
        P(("ctx", "head"), None),
    )
    return jax.shard_map(local, mesh=mesh, in_specs=in_specs, out_specs=out_specs, check_vma=False)
```

profile of v0, /device:TPU:10, one launch (start us, length us, event | category | flops | bytes accessed | tf_op | source)
XLA Modules:
  0.0 83.7 jit_solution(8443136114266541858)
XLA Ops:
  0.6 0.7 broadcast_multiply_fusion
  1.4 0.8 copy.14
  2.2 0.1 copy.13
  2.3 0.1 broadcast_in_dim.6
  2.4 1.4 %broadcast_in_dim.15.starts = s32[128,128]{1,0:T(8,128)} broadcast(s32[128]{0:T(128)} %param.15), dimensions={0} | broadcast | bytes 66048 | tf_op jit(solution)/shard_map/broadcast_in_dim | solution.py:263
  3.7 1.6 %fusion.1.kv_own = bf16[128,640]{1,0:T(8,128)(2,1)} fusion(bf16[128,64]{1,0:T(8,128)(2,1)S(1)} %copy.14, bf16[128,512]{1,0:T(8,128)(2,1)} %param.13), kind=kLoop, calls=%fused_computation.2 | loop fusion | flops 491520 | bytes 311296 | tf_op jit(solution)/shard_map/concatenate | solution.py:261
  5.3 2.1 %reshape.30 = bf16[4096,64]{1,0:T(8,128)(2,1)S(1)} reshape(bf16[128,2048]{1,0:T(8,128)(2,1)} %param.9) | data formatting | bytes 1048576 | tf_op jit(solution)/shard_map/reshape | solution.py:260
  7.4 1.2 %pad.8.qr_hbm = bf16[4096,128]{1,0:T(8,128)(2,1)} pad(bf16[4096,64]{1,0:T(8,128)(2,1)S(1)} %reshape.30, bf16[]{:T(256)} %constant.1.clone.1), padding=0_0x0_64 | pad | bytes 1572866 | tf_op jit(solution)/shard_map/jit(_pad)/pad | solution.py:260
  8.6 1.9 %broadcast_in_dim.14.lt_hbm = f32[4096,128]{1,0:T(8,128)} broadcast(f32[4096]{0:T(1024)S(1)} %broadcast_in_dim.6), dimensions={0} | broadcast | bytes 2113536 | tf_op jit(solution)/shard_map/broadcast_in_dim | solution.py:262
  10.5 62.9 %shard_map.111 = (bf16[4096,512]{1,0:T(8,128)(2,1)}, bf16[4096,128]{1,0:T(8,128)(2,1)}, bf16[64,640]{1,0:T(8,128)(2,1)}) custom-call(bf16[4096,512]{1,0:T(8,128)(2,1)} %bitcast.6, bf16[4096,128]{1,0:T(8,128)(2,1)} %pad.8.qr_hbm, bf16[4096,512]{1,0:T(8,128)(2,1)} %bitcast.7, bf16[4096,512]{1,0:T(8,128)(2,1)} %bitcast.8, f32[4096,128]{1,0:T(8,128)} %broadcast_in_dim.14.lt_hbm, ...), custom_call_target="tpu_custom_call" | custom-call | tf_op jit(solution)/shard_map/pallas_call | solution.py:267
  73.4 2.7 %reshape.34 = bf16[128,2048]{1,0:T(8,128)(2,1)} reshape(bf16[4096,64]{1,0:T(8,128)(2,1)} %bitcast.9) | data formatting | bytes 1048576 | tf_op jit(solution)/shard_map/reshape | solution.py:313
  76.1 1.3 %slice.11 = bf16[64,64]{1,0:T(8,128)(2,1)} slice(bf16[64,640]{1,0:T(8,128)(2,1)} %get-tuple-element.9), slice={[0:64], [512:576]} | slice | bytes 16384 | tf_op jit(solution)/shard_map/slice | solution.py:315
  77.4 1.5 %slice.10 = bf16[64,512]{1,0:T(8,128)(2,1)} slice(bf16[64,640]{1,0:T(8,128)(2,1)} %get-tuple-element.9), slice={[0:64], [0:512]} | slice | bytes 131072 | tf_op jit(solution)/shard_map/slice | solution.py:314
  78.9 4.8 %copy.16 = bf16[128,32,512]{2,1,0:T(8,128)(2,1)} copy(bf16[128,32,512]{2,1,0:T(8,128)(2,1)} %bitcast.5) | data formatting | bytes 8388608
where the time goes:
time: 84.1 us; the launch traced here: 83.7 us
  Pallas kernels  62.9 us (75%)
  local copies, waits for them, and re-layouts  17.8 us (21%)
  other arithmetic  2.31 us (3%)
    pallas_call x1, Pallas kernels, local(): pl.pallas_call(functools.partial(kernel, n_ctx, n_head, tok, heads, lat),...  62.9 us
    unnamed x2, local copies, waits for them, and re-layouts  5.61 us
    reshape x1, local copies, waits for them, and re-layouts, local(): gqr[:, :rope].reshape(tok, heads * rope)  2.72 us
    reshape x1, local copies, waits for them, and re-layouts, local(): qr = jnp.pad(q_rope.reshape(rows, rope), ((0, 0), (0, 128 - rope)))  2.06 us
    broadcast_in_dim x2, local copies, waits for them, and re-layouts, local(): lt = jnp.broadcast_to((log_total * LOG2E).reshape(rows, 1), (rows, 128))  2 us

commit v1 on v0

v1 whole, which is shorter than its diff:
```python
import functools

import jax
import jax.numpy as jnp
from jax import lax
from jax.experimental import pallas as pl
from jax.experimental.pallas import tpu as pltpu
from jax.sharding import PartitionSpec as P

ROPE = 64
NOPE = 128
LEVELS = 3
SPAN = 2**LEVELS
SCALE = (NOPE + ROPE) ** (-0.5)
LOG2E = 1.4426950408889634
ORDER = (1, 2, 3, 0)
BLOCK = 1024
PAIR = 2
HIDDEN = -1e30
MESH = pl.DeviceIdType.MESH


def dot_nt(a, b):
    return lax.dot_general(a, b, (((1,), (1,)), ((), ())), preferred_element_type=jnp.float32)


def dot_tn(a, b):
    return lax.dot_general(a, b, (((0,), (0,)), ((), ())), preferred_element_type=jnp.float32)


def dot_nn(a, b):
    return lax.dot_general(a, b, (((1,), (0,)), ((), ())), preferred_element_type=jnp.float32)


def kernel(
    n_ctx,
    n_head,
    tok,
    heads,
    lat,
    q_hbm,
    ao_hbm,
    go_hbm,
    q_rope,
    log_total,
    latent,
    key_rope,
    starts,
    gq_hbm,
    gqr_out,
    glat_out,
    grope_out,
    q,
    qr,
    go,
    ao,
    lt,
    delta,
    kv_own,
    kv,
    bias,
    acc,
    gacc,
    part,
    mate,
    send,
    recv,
    total,
    gq,
    gqr,
    in_sem,
    out_sem,
    kv_send,
    kv_recv,
    fw_send,
    fw_recv,
    m_send,
    m_recv,
    p_send,
    p_recv,
):
    me = lax.axis_index("ctx")
    my_head = lax.axis_index("head")
    rows = tok * heads
    block = min(BLOCK, rows)
    count = rows // block
    tok_blk = block // heads
    piece = tok // n_head
    width = PAIR * tok
    groups = SPAN // PAIR
    side = lax.rem(me, 2)
    partner = me + 1 - 2 * side
    chip = me // 2
    ahead = jnp.where(side == 0, 1, SPAN - 1)
    back = jnp.where(side == 0, SPAN - 1, 1)

    barrier = pltpu.get_barrier_semaphore()
    for dist in range(-(SPAN - 1), SPAN):
        for turn in range(n_head):
            if dist == 0 and turn == 0:
                continue

            @pl.when((me + dist >= 0) & (me + dist < n_ctx))
            def _():
                pl.semaphore_signal(
                    barrier,
                    inc=1,
                    device_id=(me + dist, lax.rem(my_head + turn, n_head)),
                    device_id_type=MESH,
                )

    def load(b):
        rng = pl.ds(b * block, block)
        return [
            pltpu.make_async_copy(src.at[rng], dst.at[rng], in_sem.at[i, b])
            for i, (src, dst) in enumerate(
                ((go_hbm, go), (ao_hbm, ao), (q_hbm, q))
            )
        ]

    for b in range(count):
        for copy in load(b):
            copy.start()

    rope_width = key_rope.shape[1]
    pair = 128 // rope_width
    key_wide = key_rope[...].astype(jnp.float32)
    kv_own[:, :lat] = latent[...]
    kv_own[:, lat:] = jnp.concatenate([key_wide] * pair, axis=1).astype(jnp.bfloat16)

    reach = jnp.minimum(me, SPAN - 1) + jnp.minimum(n_ctx - 1 - me, SPAN - 1) + 1
    pl.semaphore_wait(barrier, reach * n_head - 1)

    def tile_at(k, which):
        return pl.ds(pl.multiple_of((k * PAIR + which) * tok, tok), tok)

    def kv_copy(k):
        return pltpu.make_async_remote_copy(
            src_ref=kv_own,
            dst_ref=kv.at[tile_at(k, side)],
            send_sem=kv_send.at[k],
            recv_sem=kv_recv.at[k],
            device_id=(me + (PAIR * k if k else ahead), my_head),
            device_id_type=MESH,
        )

    def forward(k):
        return pltpu.make_async_remote_copy(
            src_ref=kv.at[tile_at(k, side)],
            dst_ref=kv.at[tile_at(k, side)],
            send_sem=fw_send.at[k],
            recv_sem=fw_recv.at[k],
            device_id=(partner, my_head),
            device_id_type=MESH,
        )

    def sends_kv(k):
        return me + (PAIR * k if k else ahead) < n_ctx

    def gets_kv(k):
        return me >= (PAIR * k if k else back)

    for k in ORDER:

        @pl.when(sends_kv(k))
        def _():
            kv_copy(k).start()

    kv[tile_at(0, side), :] = kv_own[...]

    @pl.when(me < back)
    def _():
        kv[tile_at(0, 1 - side), :] = jnp.zeros((tok, kv.shape[1]), kv.dtype)

    for k in range(1, groups):

        @pl.when(chip < k)
        def _():
            kv[pl.ds(k * width, width), :] = jnp.zeros((width, kv.shape[1]), kv.dtype)

    def pass_on(k):
        if k:

            @pl.when(gets_kv(k))
            def _():
                kv_copy(k).wait_recv()
                forward(k).start()

    part_of = lax.broadcasted_iota(jnp.int32, (tok, 128), 1) // rope_width
    for head in range(heads):
        lanes = pl.ds((head // pair) * 128, 128)
        own = jnp.where(part_of == head % pair, q_rope[:, lanes].astype(jnp.float32), 0.0)
        qr[pl.ds(head, tok, stride=heads), :] = own
    lt_wide = jnp.broadcast_to((log_total[...] * LOG2E)[:, :, None], (tok, heads, 128))
    lt[...] = lt_wide.reshape(rows, 128)
    first = jnp.broadcast_to(starts[...].astype(jnp.float32), (tok, tok)).T.astype(jnp.int32)
    query_pos = me * tok + lax.broadcasted_iota(jnp.int32, (tok, tok), 0)
    lane = lax.broadcasted_iota(jnp.int32, (tok, tok), 1)
    for k in range(groups):
        for which in range(PAIR):
            tile = PAIR * (chip - k) + which
            if k == 0 and which:
                tile = jnp.where(side == 0, me - (SPAN - 1), me)
            key_pos = tile * tok + lane
            seen = (key_pos >= first) & (key_pos <= query_pos)
            bias[k, :, pl.ds(which * tok, tok)] = jnp.where(seen, 0.0, HIDDEN)

    def mate_copy(k):
        return pltpu.make_async_remote_copy(
            src_ref=part.at[tile_at(k, 1 - side)],
            dst_ref=mate.at[k],
            send_sem=m_send.at[k],
            recv_sem=m_recv.at[k],
            device_id=(partner, my_head),
            device_id_type=MESH,
        )

    def part_copy(k, turn):
        target = lax.rem(my_head + turn, n_head)
        if k in (0, groups):
            which = side if k == 0 else 1 - side
            src = part.at[pl.ds(pl.multiple_of(which * tok + target * piece, piece), piece)]
        else:
            src = send.at[k, pl.ds(pl.multiple_of(target * piece, piece), piece)]
        return pltpu.make_async_remote_copy(
            src_ref=src,
            dst_ref=recv.at[k * n_head + turn],
            send_sem=p_send.at[k * n_head + turn],
            recv_sem=p_recv.at[k * n_head + turn],
            device_id=(me - (back if k == groups else PAIR * k), target),
            device_id_type=MESH,
        )

    def sends_part(k):
        return me >= (back if k == groups else PAIR * k)

    def gets_part(k):
        return me + (ahead if k == groups else PAIR * k) < n_ctx

    def start_parts(k):
        for turn in range(n_head):
            if k or turn:

                @pl.when(sends_part(k))
                def _():
                    part_copy(k, turn).start()

    def join(k):
        @pl.when(sends_part(k))
        def _():
            mate_copy(k).wait_recv()
            own = part[tile_at(k, side), :].astype(jnp.float32)
            send[k] = (own + mate[k].astype(jnp.float32)).astype(jnp.bfloat16)

        start_parts(k)

    def row_delta(b, unused):
        rng = pl.ds(pl.multiple_of(b * block, block), block)
        for copy in load(b):
            copy.wait()
        d = jnp.sum(
            go[rng, :].astype(jnp.float32) * ao[rng, :].astype(jnp.float32), axis=1, keepdims=True
        )
        delta[rng, :] = jnp.broadcast_to(d * SCALE, (block, 128))
        return unused

    lax.fori_loop(0, count, row_delta, 0)
    pass_on(ORDER[0])
    mid = min(1, count - 1)
    for turn_at, k in enumerate(ORDER):
        earlier = ORDER[turn_at - 1] if turn_at else None
        later = ORDER[turn_at + 1] if turn_at < groups - 1 else None

        @pl.when(gets_kv(k))
        def _():
            if k:
                forward(k).wait_recv()
            else:
                kv_copy(k).wait_recv()

        gacc[...] = jnp.zeros_like(gacc)

        def step(b, unused):
            start = pl.multiple_of(b * block, block)
            rng = pl.ds(start, block)

            @pl.when(b == mid)
            def _():
                if later is not None:
                    pass_on(later)
                if earlier:
                    join(earlier)

            keys = kv[pl.ds(k * width, width), :]
            q_b, qr_b, go_b = q[rng, :], qr[rng, :].astype(jnp.bfloat16), go[rng, :]
            scores = dot_nt(q_b, keys[:, :lat]) + dot_nt(qr_b, keys[:, lat:])
            grad_probs = dot_nt(go_b, keys[:, :lat])
            hide = bias[k, pl.ds(pl.multiple_of(b * tok_blk, tok_blk), tok_blk), :]
            hide = jnp.broadcast_to(hide[:, None, :], (tok_blk, heads, width)).reshape(block, width)
            times = width // 128
            lt_b = jnp.concatenate([lt[rng, :]] * times, axis=1)
            d_b = jnp.concatenate([delta[rng, :]] * times, axis=1)
            probs = jnp.exp2(scores * (SCALE * LOG2E) - lt_b + hide)
            grads = probs * (grad_probs * SCALE - d_b)
            probs_b = probs.astype(jnp.bfloat16)
            grad_b = grads.astype(jnp.bfloat16)
            gq_b = dot_nn(grad_b, keys)
            if earlier is not None:
                gq_b = acc[rng, :] + gq_b
            if later is not None:
                acc[rng, :] = gq_b
            else:
                gq[rng, :] = gq_b[:, :lat].astype(jnp.bfloat16)
                gqr[rng, :] = gq_b[:, lat:]
                pltpu.make_async_copy(gq.at[rng], gq_hbm.at[rng], out_sem.at[b]).start()
            gacc[:, :lat] += dot_tn(probs_b, go_b) + dot_tn(grad_b, q_b)
            gacc[:, lat:] += dot_tn(grad_b, qr_b)
            return unused

        lax.fori_loop(0, count, step, 0)
        part[pl.ds(k * width, width), :] = gacc[...].astype(jnp.bfloat16)
        if k:

            @pl.when(sends_part(k))
            def _():
                mate_copy(k).start()

        else:
            start_parts(groups)
            start_parts(0)
    if ORDER[-1]:
        join(ORDER[-1])

    for tile in range(heads // pair):
        own = gqr[pl.ds(tile * pair, tok, stride=heads), :]
        for i in range(1, pair):
            own = jnp.where(part_of == i, gqr[pl.ds(tile * pair + i, tok, stride=heads), :], own)
        gqr_out[:, pl.ds(tile * 128, 128)] = own.astype(jnp.bfloat16)

    mine = pl.ds(pl.multiple_of(side * tok + my_head * piece, piece), piece)
    total[...] = part[mine, :].astype(jnp.float32)
    for k in ORDER[:-1] + (ORDER[-1], groups):
        for turn in range(n_head):
            if k or turn:

                @pl.when(gets_part(k))
                def _():
                    part_copy(k, turn).wait_recv()
                    total[...] += recv[k * n_head + turn].astype(jnp.float32)

    glat_out[...] = total[:, :lat].astype(jnp.bfloat16)
    rope_sum = total[:, lat : lat + rope_width]
    for i in range(1, pair):
        rope_sum += total[:, lat + i * rope_width : lat + (i + 1) * rope_width]
    grope_out[...] = rope_sum.astype(jnp.bfloat16)
    for k in range(groups):

        @pl.when(sends_kv(k))
        def _():
            kv_copy(k).wait_send()

        if k:

            @pl.when(gets_kv(k))
            def _():
                forward(k).wait_send()
                mate_copy(k).wait_send()

    for k in range(groups + 1):
        for turn in range(n_head):
            if k or turn:

                @pl.when(sends_part(k))
                def _():
                    part_copy(k, turn).wait_send()

    for b in range(count):
        rng = pl.ds(b * block, block)
        pltpu.make_async_copy(gq.at[rng], gq_hbm.at[rng], out_sem.at[b]).wait()


def local(q_latent, q_rope, attn_out, grad_out, log_total, latent, key_rope, doc_start):
    n_ctx, n_head = lax.axis_size("ctx"), lax.axis_size("head")
    tok, heads, lat = q_latent.shape
    rows = tok * heads
    rope = key_rope.shape[1]
    wide = lat + 128
    block = min(BLOCK, rows)
    count = rows // block
    piece = tok // n_head
    width = PAIR * tok
    slots = (SPAN // PAIR + 1) * n_head
    bf, f32 = jnp.bfloat16, jnp.float32
    hbm = pl.BlockSpec(memory_space=pl.ANY)
    vmem = pl.BlockSpec(memory_space=pltpu.VMEM)
    gq, gqr, glat, grope = pl.pallas_call(
        functools.partial(kernel, n_ctx, n_head, tok, heads, lat),
        out_shape=(
            jax.ShapeDtypeStruct((rows, lat), bf),
            jax.ShapeDtypeStruct(q_rope.shape, bf),
            jax.ShapeDtypeStruct((piece, lat), bf),
            jax.ShapeDtypeStruct((piece, rope), bf),
        ),
        in_specs=[hbm] * 3 + [vmem] * 5,
        out_specs=(hbm, vmem, vmem, vmem),
        scratch_shapes=[
            pltpu.VMEM((rows, lat), bf),
            pltpu.VMEM((rows, 128), f32),
            pltpu.VMEM((rows, lat), bf),
            pltpu.VMEM((rows, lat), bf),
            pltpu.VMEM((rows, 128), f32),
            pltpu.VMEM((rows, 128), f32),
            pltpu.VMEM((tok, wide), bf),
            pltpu.VMEM((SPAN * tok, wide), bf),
            pltpu.VMEM((SPAN // PAIR, tok, width), f32),
            pltpu.VMEM((rows, wide), f32),
            pltpu.VMEM((width, wide), f32),
            pltpu.VMEM((SPAN * tok, wide), bf),
            pltpu.VMEM((SPAN // PAIR, tok, wide), bf),
            pltpu.VMEM((SPAN // PAIR, tok, wide), bf),
            pltpu.VMEM((slots, piece, wide), bf),
            pltpu.VMEM((piece, wide), f32),
            pltpu.VMEM((rows, lat), bf),
            pltpu.VMEM((rows, 128), f32),
            pltpu.SemaphoreType.DMA((3, count)),
            pltpu.SemaphoreType.DMA((count,)),
            pltpu.SemaphoreType.DMA((SPAN // PAIR,)),
            pltpu.SemaphoreType.DMA((SPAN // PAIR,)),
            pltpu.SemaphoreType.DMA((SPAN // PAIR,)),
            pltpu.SemaphoreType.DMA((SPAN // PAIR,)),
            pltpu.SemaphoreType.DMA((SPAN // PAIR,)),
            pltpu.SemaphoreType.DMA((SPAN // PAIR,)),
            pltpu.SemaphoreType.DMA((slots,)),
            pltpu.SemaphoreType.DMA((slots,)),
        ],
        compiler_params=pltpu.CompilerParams(
            collective_id=0, has_side_effects=True, vmem_limit_bytes=56 * 2**20
        ),
    )(
        q_latent.reshape(rows, lat),
        attn_out.reshape(rows, lat),
        grad_out.reshape(rows, lat),
        q_rope,
        log_total,
        latent,
        key_rope,
        doc_start.reshape(1, tok),
    )
    return gq.reshape(tok, heads, lat), gqr, glat, grope


def solution(mesh):
    in_specs = (
        P("ctx", "head", None),
        P("ctx", "head"),
        P("ctx", "head", None),
        P("ctx", "head", None),
        P("ctx", "head"),
        P("ctx", None),
        P("ctx", None),
        P("ctx"),
    )
    out_specs = (
        P("ctx", "head", None),
        P("ctx", "head"),
        P(("ctx", "head"), None),
        P(("ctx", "head"), None),
    )
    return jax.shard_map(local, mesh=mesh, in_specs=in_specs, out_specs=out_specs, check_vma=False)
```

time: 84.1 us -> 68.4 us (0.81)
  the two profiles are of different devices: /device:TPU:10 before, /device:TPU:3 now
where the time goes in v1:
time: 68.4 us; the launch traced here: 68.1 us
  Pallas kernels  57.7 us (84%)
  local copies, waits for them, and re-layouts  9.77 us (14%)
    pallas_call x1, Pallas kernels, local(): pl.pallas_call(functools.partial(kernel, n_ctx, n_head, tok, heads, lat),...  57.7 us
    unnamed x12, local copies, waits for them, and re-layouts  9.77 us

profile of v1, /device:TPU:3, one launch (start us, length us, event | category | flops | bytes accessed | tf_op | source)
XLA Modules:
  0.0 68.1 jit_solution(772919449760749931)
XLA Ops:
  0.6 1.4 %copy.13.key_rope = bf16[128,64]{1,0:T(8,128)(2,1)} copy(bf16[128,64]{0,1:T(8,128)(2,1)} %param.14) | data formatting | bytes 32768 | tf_op args[6]
  2.1 1.4 %copy.12.log_total = f32[128,32]{1,0:T(8,128)} copy(f32[128,32]{0,1:T(8,128)} %param.12) | data formatting | bytes 32768 | tf_op args[4]
  3.5 57.7 %shard_map.111 = (bf16[4096,512]{1,0:T(8,128)(2,1)}, bf16[128,2048]{1,0:T(8,128)(2,1)}, bf16[64,512]{1,0:T(8,128)(2,1)}, bf16[64,64]{1,0:T(8,128)(2,1)}) custom-call(bf16[4096,512]{1,0:T(8,128)(2,1)} %bitcast.6, bf16[4096,512]{1,0:T(8,128)(2,1)} %bitcast.7, bf16[4096,512]{1,0:T(8,128)(2,1)} %bitcast.8, bf16[128,2048]{1,0:T(8,128)(2,1)} %q_rope.1, ...), custom_call_target="tpu_custom_call" | custom-call | tf_op jit(solution)/shard_map/pallas_call | solution.py:396
  61.2 0.0 copy-start
  61.2 0.0 copy-start.1
  61.2 0.0 copy-start.2
  61.2 4.8 %copy.18 = bf16[128,32,512]{2,1,0:T(8,128)(2,1)} copy(bf16[128,32,512]{2,1,0:T(8,128)(2,1)} %bitcast.5) | data formatting | bytes 8388608
  66.1 0.0 copy-done
  66.1 0.8 %copy.19 = bf16[128,2048]{1,0:T(8,128)(2,1)} copy(bf16[128,2048]{1,0:T(8,128)(2,1)S(1)} %copy-done) | data formatting | bytes 1048576
  66.9 0.0 copy-done.1
  66.9 0.6 copy.20
  67.5 0.0 copy-done.2
  67.5 0.6 copy.21
Async XLA Ops:
  61.2 4.9 %copy-start = (bf16[128,2048]{1,0:T(8,128)(2,1)S(1)}, bf16[128,2048]{1,0:T(8,128)(2,1)}, u32[]{:S(2)}) copy-start(bf16[128,2048]{1,0:T(8,128)(2,1)} %get-tuple-element.17) | copy-start | bytes 1572868
  61.2 5.7 %copy-start.1 = (bf16[64,512]{1,0:T(8,128)(2,1)S(1)}, bf16[64,512]{1,0:T(8,128)(2,1)}, u32[]{:S(2)}) copy-start(bf16[64,512]{1,0:T(8,128)(2,1)} %get-tuple-element.18) | copy-start | bytes 196612
  61.2 6.3 %copy-start.2 = (bf16[64,64]{1,0:T(8,128)(2,1)S(1)}, bf16[64,64]{1,0:T(8,128)(2,1)}, u32[]{:S(2)}) copy-start(bf16[64,64]{1,0:T(8,128)(2,1)} %get-tuple-element.19) | copy-start | bytes 24580

commit v2 on v1

--- a/solution.py
+++ b/solution.py
@@ -14,7 +14,7 @@
 SCALE = (NOPE + ROPE) ** (-0.5)
 LOG2E = 1.4426950408889634
 ORDER = (1, 2, 3, 0)
-BLOCK = 1024
+BLOCK = 2048
 PAIR = 2
 HIDDEN = -1e30
 MESH = pl.DeviceIdType.MESH
@@ -122,9 +122,9 @@
         for copy in load(b):
             copy.start()
 
-    rope_width = key_rope.shape[1]
+    rope_width = key_rope.shape[0]
     pair = 128 // rope_width
-    key_wide = key_rope[...].astype(jnp.float32)
+    key_wide = key_rope[...].astype(jnp.float32).T
     kv_own[:, :lat] = latent[...]
     kv_own[:, lat:] = jnp.concatenate([key_wide] * pair, axis=1).astype(jnp.bfloat16)
 
@@ -191,7 +191,7 @@
         lanes = pl.ds((head // pair) * 128, 128)
         own = jnp.where(part_of == head % pair, q_rope[:, lanes].astype(jnp.float32), 0.0)
         qr[pl.ds(head, tok, stride=heads), :] = own
-    lt_wide = jnp.broadcast_to((log_total[...] * LOG2E)[:, :, None], (tok, heads, 128))
+    lt_wide = jnp.broadcast_to((log_total[...] * LOG2E).T[:, :, None], (tok, heads, 128))
     lt[...] = lt_wide.reshape(rows, 128)
     first = jnp.broadcast_to(starts[...].astype(jnp.float32), (tok, tok)).T.astype(jnp.int32)
     query_pos = me * tok + lax.broadcasted_iota(jnp.int32, (tok, tok), 0)
@@ -441,9 +441,9 @@
         attn_out.reshape(rows, lat),
         grad_out.reshape(rows, lat),
         q_rope,
-        log_total,
+        log_total.T,
         latent,
-        key_rope,
+        key_rope.T,
         doc_start.reshape(1, tok),
     )
     return gq.reshape(tok, heads, lat), gqr, glat, grope

time: 68.4 us -> 64 us (0.936)
  the two profiles are of different devices: /device:TPU:3 before, /device:TPU:1 now
where the time goes in v2:
time: 64 us; the launch traced here: 63.8 us
  Pallas kernels  56.2 us (88%)
  local copies, waits for them, and re-layouts  6.89 us (11%)
  between operations  0.67 us (1%)
    pallas_call x1, Pallas kernels, local(): pl.pallas_call(functools.partial(kernel, n_ctx, n_head, tok, heads, lat),...  56.2 us
    unnamed x10, local copies, waits for them, and re-layouts  6.89 us

profile of v2, /device:TPU:1, one launch (start us, length us, event | category | flops | bytes accessed | tf_op | source)
XLA Modules:
  0.0 63.8 jit_solution(5216809374549649467)
XLA Ops:
  0.6 56.2 %shard_map.111 = (bf16[4096,512]{1,0:T(8,128)(2,1)}, bf16[128,2048]{1,0:T(8,128)(2,1)}, bf16[64,512]{1,0:T(8,128)(2,1)}, bf16[64,64]{1,0:T(8,128)(2,1)}) custom-call(bf16[4096,512]{1,0:T(8,128)(2,1)} %bitcast.7, bf16[4096,512]{1,0:T(8,128)(2,1)} %bitcast.8, bf16[4096,512]{1,0:T(8,128)(2,1)} %bitcast.9, bf16[128,2048]{1,0:T(8,128)(2,1)} %q_rope.1, ...), custom_call_target="tpu_custom_call" | custom-call | tf_op jit(solution)/shard_map/pallas_call | solution.py:396
  56.9 0.0 copy-start
  56.9 0.0 copy-start.1
  56.9 0.0 copy-start.2
  56.9 4.8 %copy.16 = bf16[128,32,512]{2,1,0:T(8,128)(2,1)} copy(bf16[128,32,512]{2,1,0:T(8,128)(2,1)} %bitcast.10) | data formatting | bytes 8388608
  61.8 0.0 copy-done
  61.8 0.8 %copy.17 = bf16[128,2048]{1,0:T(8,128)(2,1)} copy(bf16[128,2048]{1,0:T(8,128)(2,1)S(1)} %copy-done) | data formatting | bytes 1048576
  62.6 0.0 copy-done.1
  62.6 0.6 copy.18
  63.2 0.0 copy-done.2
  63.2 0.6 copy.19
Async XLA Ops:
  56.9 4.9 %copy-start = (bf16[128,2048]{1,0:T(8,128)(2,1)S(1)}, bf16[128,2048]{1,0:T(8,128)(2,1)}, u32[]{:S(2)}) copy-start(bf16[128,2048]{1,0:T(8,128)(2,1)} %get-tuple-element.17) | copy-start | bytes 1572868
  56.9 5.7 %copy-start.1 = (bf16[64,512]{1,0:T(8,128)(2,1)S(1)}, bf16[64,512]{1,0:T(8,128)(2,1)}, u32[]{:S(2)}) copy-start(bf16[64,512]{1,0:T(8,128)(2,1)} %get-tuple-element.18) | copy-start | bytes 196612
  56.9 6.3 %copy-start.2 = (bf16[64,64]{1,0:T(8,128)(2,1)S(1)}, bf16[64,64]{1,0:T(8,128)(2,1)}, u32[]{:S(2)}) copy-start(bf16[64,64]{1,0:T(8,128)(2,1)} %get-tuple-element.19) | copy-start | bytes 24580
